TPU v7x, 32 devices: a whole 2x2x4 slice. The times are simulated.
32 devices in a mesh: row: 8 (over z, x), col: 4 (over y, core).
Axes of the slice: x: 2, y: 2, z: 4, core: 2. Of those that a mesh axis runs over, the one named last changes fastest.
Arguments:
- hidden: bfloat16 [8192, 1600], P('row', 'col'), may hold values from -60 to 60
- up_weight: bfloat16 [1600, 6400], P('row', 'col'), may hold values from -0.15625 to 0.15625
- up_bias: float32 [6400], P('col'), may hold values from -3 to 3
- down_weight: bfloat16 [6400, 1600], P('col', 'row'), may hold values from -0.078125 to 0.078125
- down_bias: float32 [1600], P('col'), may hold values from -3 to 3
- query_key_value_weight: bfloat16 [1600, 4800], P('row', 'col'), may hold values from -0.15625 to 0.15625
- query_key_value_bias: float32 [4800], P('col'), may hold values from -3 to 3
- block_norm_gain: float32 [1600], replicated, may hold values from 0.1 to 1.9
- block_norm_shift: float32 [1600], replicated, may hold values from -3 to 3
- following_norm_gain: float32 [1600], replicated, may hold values from 0.1 to 1.9
- following_norm_shift: float32 [1600], replicated, may hold values from -3 to 3
- up_down_factors: bfloat16 [32, 16, 1600], P('row'), may hold values from -0.15625 to 0.15625
- up_up_factors: bfloat16 [32, 16, 6400], P('row', None, 'col'), may hold values from -1.5 to 1.5
- query_key_value_down_factors: bfloat16 [32, 16, 1600], P('row'), may hold values from -0.15625 to 0.15625
- query_key_value_up_factors: bfloat16 [32, 16, 4800], P('row', None, 'col'), may hold values from -1.5 to 1.5
- adapter_storage_slot: int32 [32], replicated, may hold values from 0 to 31, as said below
- tile_adapter_index: int32 [64], P('row'), may hold values from 0 to 31, as said below
- tile_token_rows: int32 [64], P('row'), may hold values from 1 to 128, as said below
Outputs:
- h_out: bfloat16 [8192, 1600], P('row', 'col')
- qkv: bfloat16 [8192, 4800], P('row', 'col')
Inputs may be any that keep to these rules, and one draw needn't show every extreme that they name: A permutation: adapter a is stored in slot adapter_storage_slot[a], and index r of row holds slots r * 4 to (r + 1) * 4 - 1. `tile_adapter_index`: the 8 tiles of one index of row name adapters whose slots lie on distinct indices of row. A tile's first tile_token_rows rows are prompt tokens, the rest padding.
All inputs are finite; a program needn't handle non-finite values.
Results may differ from a plain program's by a relative error of at most 0.02.
Values may be sent and summed in bfloat16 or wider, within the bound.
A program may use at most 64 MiB of HBM per device.

v0:
```python
import jax
import jax.numpy as jnp
from jax import lax
from jax.sharding import PartitionSpec as P


def layer_norm(values, gain_vec, shift_vec):
    row_mean = jnp.mean(values, axis=-1, keepdims=True)
    centred = values - row_mean
    variance = jnp.mean(centred * centred, axis=-1, keepdims=True)
    return centred * lax.rsqrt(variance + 1e-05) * gain_vec + shift_vec


def fold_rows(operand, weight_piece):
    return jnp.dot(operand, weight_piece, preferred_element_type=jnp.float32)


def adapter_update(
    normalized_input, down_factor, up_factor, holder_row, resident_slot, tile_total_count
):
    tok_rows, feat_width = normalized_input.shape
    tile_len = tok_rows // tile_total_count
    per_holder, adapter_rank_size, unused_result = down_factor.shape
    tiled_rows = normalized_input.reshape(tile_total_count, tile_len, feat_width)
    owners = lax.axis_size("row")
    select = (holder_row[None, :] == jnp.arange(owners, dtype=jnp.int32)[:, None]).astype(
        jnp.bfloat16
    )
    slot_pick = (resident_slot[:, None] == jnp.arange(per_holder, dtype=jnp.int32)[None, :]).astype(
        jnp.bfloat16
    )
    outgoing = jnp.einsum(
        "ot,tid->oid", select, tiled_rows, preferred_element_type=jnp.float32
    ).astype(jnp.bfloat16)
    labels = jnp.dot(select, slot_pick, preferred_element_type=jnp.float32).astype(jnp.bfloat16)
    received_rows, slot_marks = (
        lax.all_to_all(outgoing, "row", split_axis=0, concat_axis=0, tiled=True),
        lax.all_to_all(labels, "row", split_axis=0, concat_axis=0, tiled=True),
    )
    every_low_rank = jnp.einsum(
        "kph,fch->kpfc", received_rows, down_factor, preferred_element_type=jnp.float32
    )
    low_rank = jnp.sum(
        every_low_rank * slot_marks.astype(jnp.float32)[:, None, :, None], axis=2
    ).astype(jnp.bfloat16)
    broadcast_rows = (low_rank[:, :, None, :] * slot_marks[:, None, :, None]).reshape(
        owners, tile_len, per_holder * adapter_rank_size
    )
    answer = jnp.einsum(
        "sik,kf->sif",
        broadcast_rows,
        up_factor.reshape(per_holder * adapter_rank_size, -1),
        preferred_element_type=jnp.float32,
    ).astype(jnp.bfloat16)
    returned = lax.all_to_all(answer, "row", split_axis=0, concat_axis=0, tiled=True)
    update_rows = jnp.einsum(
        "ot,oif->tif", select, returned, preferred_element_type=jnp.float32
    ).astype(jnp.bfloat16)
    update_rows = lax.optimization_barrier(update_rows)
    return update_rows.reshape(tok_rows, -1).astype(jnp.float32)


def per_device(
    hidden,
    up_weight,
    up_bias,
    down_weight,
    down_bias,
    query_key_value_weight,
    query_key_value_bias,
    block_norm_gain,
    block_norm_shift,
    following_norm_gain,
    following_norm_shift,
    up_down_factors,
    up_up_factors,
    query_key_value_down_factors,
    query_key_value_up_factors,
    adapter_storage_slot,
    tile_adapter_index,
    tile_token_rows,
):
    tok_rows = hidden.shape[0]
    tile_total_count = tile_adapter_index.shape[0]
    tile_len = tok_rows // tile_total_count
    per_holder = up_down_factors.shape[0]
    adapter_count = adapter_storage_slot.shape[0]
    adapter_pick = (
        tile_adapter_index[:, None] == jnp.arange(adapter_count, dtype=jnp.int32)[None, :]
    ).astype(jnp.int32)
    slot_ids = jnp.sum(adapter_pick * adapter_storage_slot[None, :], axis=1)
    holder_row = slot_ids // per_holder
    resident_slot = slot_ids % per_holder
    valid = (jnp.arange(tile_len, dtype=jnp.int32)[None, :] < tile_token_rows[:, None]).reshape(
        tok_rows, 1
    )
    gathered = lax.all_gather(hidden, "col", axis=1, tiled=True)
    normalized_input = layer_norm(
        gathered.astype(jnp.float32), block_norm_gain, block_norm_shift
    ).astype(jnp.bfloat16)
    up_dense = fold_rows(normalized_input, lax.all_gather(up_weight, "row", axis=0, tiled=True))
    up_projection = (
        up_dense
        + up_bias
        + adapter_update(
            normalized_input,
            up_down_factors,
            up_up_factors,
            holder_row,
            resident_slot,
            tile_total_count,
        )
    )
    activated = jax.nn.gelu(up_projection, approximate=True).astype(jnp.bfloat16)
    partial_value = jnp.dot(
        activated,
        lax.all_gather(down_weight, "row", axis=1, tiled=True),
        preferred_element_type=jnp.float32,
    )
    summed = lax.psum_scatter(
        partial_value.astype(jnp.bfloat16), "col", scatter_dimension=1, tiled=True
    ).astype(jnp.float32)
    mixed = hidden.astype(jnp.float32) + summed + down_bias
    h_out = jnp.where(valid, mixed, 0.0).astype(jnp.bfloat16)
    gathered_next = lax.all_gather(h_out, "col", axis=1, tiled=True)
    normalized_following = layer_norm(
        gathered_next.astype(jnp.float32), following_norm_gain, following_norm_shift
    ).astype(jnp.bfloat16)
    qkv_dense = fold_rows(
        normalized_following, lax.all_gather(query_key_value_weight, "row", axis=0, tiled=True)
    )
    projected_output = (
        qkv_dense
        + query_key_value_bias
        + adapter_update(
            normalized_following,
            query_key_value_down_factors,
            query_key_value_up_factors,
            holder_row,
            resident_slot,
            tile_total_count,
        )
    )
    qkv = jnp.where(valid, projected_output, 0.0).astype(jnp.bfloat16)
    return (h_out, qkv)


def solution(mesh):
    in_specs = (
        P("row", "col"),
        P("row", "col"),
        P("col"),
        P("col", "row"),
        P("col"),
        P("row", "col"),
        P("col"),
        P(),
        P(),
        P(),
        P(),
        P("row", None, None),
        P("row", None, "col"),
        P("row", None, None),
        P("row", None, "col"),
        P(),
        P("row"),
        P("row"),
    )
    out_specs = (P("row", "col"), P("row", "col"))
    return jax.shard_map(
        per_device, mesh=mesh, in_specs=in_specs, out_specs=out_specs, check_vma=False
    )
```

profile of v0, /device:TPU:0, one launch (start us, length us, event | category | flops | bytes accessed | tf_op | source)
XLA Modules:
  0.0 654.0 jit_solution(14058357577489934825)
XLA Ops:
  7.2 0.7 all-gather.6.cloned.1.call-update
  8.0 0.7 all-gather.8.cloned.1.call-update
  8.7 0.9 select_reduce_fusion
  9.6 0.3 fusion.48
  9.8 0.7 copy.30
  10.5 7.3 %all-to-all-start.1 = ((bf16[8,1,4]{2,1,0:T(2,128)(2,1)}), bf16[8,1,4]{2,1,0:T(2,128)(2,1)S(1)}, u32[]{:S(2)}, u32[]{:S(2)}) async-start(bf16[8,1,4]{2,1,0:T(2,128)(2,1)} %copy.30), calls=%async_computation.1 | async-start | bytes 8192 | tf_op jit(solution)/shard_map/all_to_all | solution.py:38
  17.8 23.9 %all-gather.6.cloned.1.call-done = bf16[1024,1600]{0,1:T(8,128)(2,1)} async-done(((bf16[1024,400]{0,1:T(8,128)(2,1)}), bf16[1024,1600]{0,1:T(8,128)(2,1)}) %all-gather.6.cloned.1.call-update) | async-done | bytes 3276816 | tf_op jit(solution)/shard_map/all_gather | solution.py:97
  41.6 2.7 convert_reduce_fusion.1
  44.3 0.2 copy-done.2
  44.5 0.9 fusion.8
  45.5 1.6 fusion.75
  47.1 0.9 copy.46
  48.0 1.4 convolution_convert_fusion.2
  49.4 2.3 copy.29
  51.7 5.5 all-to-all-start
  57.2 0.7 all-gather.10.cloned.1.call-update
  58.0 0.1 copy.31
  58.1 0.1 copy.32
  58.1 0.1 copy.33
  58.2 127.9 %all-to-all-done = bf16[8,128,1600]{1,2,0:T(8,128)(2,1)} async-done(((bf16[8,128,1600]{1,2,0:T(8,128)(2,1)}), bf16[8,128,1600]{1,2,0:T(8,128)(2,1)}, u32[]{:S(2)}, u32[]{:S(2)}) %all-to-all-start) | async-done | bytes 3276832 | tf_op jit(solution)/shard_map/all_to_all | solution.py:37
  186.1 2.6 fusion.45
  188.8 1.1 bitcast_convert_fusion
  189.9 138.7 %all_to_all.33 = bf16[8,128,1600]{1,2,0:T(8,128)(2,1)S(1)} all-to-all(bf16[8,128,1600]{1,2,0:T(8,128)(2,1)S(1)} %bitcast_convert_fusion), channel_id=1, replica_groups=mesh['row'=8,'col'=4] {'row'}, dimensions={0} | all-to-all | bytes 6553600 | tf_op jit(solution)/shard_map/all_to_all | solution.py:55
  328.5 2.0 fusion.30
  330.6 2.9 convert_element_type.115
  333.5 14.9 %fusion.19.clone.4 = bf16[1024,1600]{0,1:T(8,128)(2,1)} fusion(f32[200,8,8,128]{3,2,1,0:T(8,128)} %bitcast.93, bf16[1600,1600]{1,0:T(8,128)(2,1)} %all-gather.8.cloned.1.call-done, f32[1600]{0:T(1024)S(1)} %copy-done.11, bf16[1024,1600]{0,1:T(8,128)(2,1)S(1)} %copy-done.2, f32[1600]{0:T(1024)S(1)} %copy-done.6, f32[1600]{0:T(1024)S(1)} %copy-done.7, ...), kind=kOutput, calls=%fused_computation.24.clone.clone.clone.1 | convolution fusion | flops 5270732800 | bytes 18254592 | tf_op jit(solution)/shard_map/dot_general | solution.py:15
  348.4 10.8 %convolution_convert_fusion = bf16[1024,1600]{0,1:T(8,128)(2,1)} fusion(bf16[1600,1600]{0,1:T(8,128)(2,1)} %all-gather.10.cloned.1.call-done, bf16[1024,1600]{0,1:T(8,128)(2,1)} %fusion.19.clone.4), kind=kOutput, calls=%fused_computation.31 | convolution fusion | flops 5244518400 | bytes 11673600 | tf_op jit(solution)/shard_map/dot_general | solution.py:115
  359.3 0.0 all-gather.12.cloned.1.call-start
  359.3 0.1 fusion.64
  359.4 38.2 %reduce-scatter.2.cloned.1.call-done = bf16[1024,400]{0,1:T(8,128)(2,1)} async-done(((bf16[1024,1600]{0,1:T(8,128)(2,1)}), bf16[1024,400]{0,1:T(8,128)(2,1)}) %reduce-scatter.2.cloned.1.call-update) | async-done | bytes 819216 | tf_op jit(solution)/shard_map/reduce_scatter | solution.py:120
  397.7 2.3 select_convert_fusion
  400.0 29.4 %all-gather.12.cloned.1.call-done = bf16[1024,1600]{0,1:T(8,128)(2,1)} async-done(((bf16[1024,400]{0,1:T(8,128)(2,1)}), bf16[1024,1600]{0,1:T(8,128)(2,1)}) %all-gather.12.cloned.1.call-update) | async-done | bytes 3276816 | tf_op jit(solution)/shard_map/all_gather | solution.py:125
  429.5 2.7 convert_reduce_fusion
  432.2 0.2 copy-done.3
  432.4 0.9 fusion.4
  433.3 1.6 fusion.78
  435.0 0.9 copy.48
  435.8 1.4 convolution_convert_fusion.1
  437.3 2.2 copy.36
  439.5 5.6 all-to-all-start.3
  445.2 0.5 all-gather.14.cloned.1.call-update
  445.7 123.2 %all-to-all-done.3 = bf16[8,128,1600]{1,2,0:T(8,128)(2,1)} async-done(((bf16[8,128,1600]{1,2,0:T(8,128)(2,1)}), bf16[8,128,1600]{1,2,0:T(8,128)(2,1)}, u32[]{:S(2)}, u32[]{:S(2)}) %all-to-all-start.3) | async-done | bytes 3276832 | tf_op jit(solution)/shard_map/all_to_all | solution.py:37
  568.9 2.6 fusion.42
  571.6 1.8 bitcast_convert_fusion.1
  573.4 59.6 %all_to_all.34 = bf16[8,128,1200]{1,2,0:T(8,128)(2,1)S(1)} all-to-all(bf16[8,128,1200]{1,2,0:T(8,128)(2,1)S(1)} %bitcast_convert_fusion.1), channel_id=1, replica_groups=mesh['row'=8,'col'=4] {'row'}, dimensions={0} | all-to-all | bytes 4915200 | tf_op jit(solution)/shard_map/all_to_all | solution.py:55
  633.0 0.8 fusion.33
  633.9 2.4 convert_element_type.116
  636.3 10.9 %fusion.21 = bf16[1024,1200]{0,1:T(8,128)(2,1)} fusion(f32[150,8,8,128]{3,2,1,0:T(8,128)} %bitcast.94, bf16[1600,1200]{1,0:T(8,128)(2,1)} %all-gather.14.cloned.1.call-done, f32[1200]{0:T(1024)S(1)} %copy-done.12, pred[1024]{0:T(1024)(128)(4,1)S(1)} %fusion.64, bf16[1024,1600]{0,1:T(8,128)(2,1)S(1)} %copy-done.3, f32[1600]{0:T(1024)S(1)} %copy-done.8, ...), kind=kOutput, calls=%fused_computation.29 | convolution fusion | flops 3946905600 | bytes 14516416 | tf_op jit(solution)/shard_map/dot_general | solution.py:15
  (43 shorter events, 0.3 us)
Async XLA Ops:
  7.2 181.6 %copy-start = (bf16[4,16,1600]{2,1,0:T(8,128)(2,1)S(1)}, bf16[4,16,1600]{2,1,0:T(8,128)(2,1)}, u32[]{:S(2)}) copy-start(bf16[4,16,1600]{2,1,0:T(8,128)(2,1)} %param.30) | copy-start | bytes 614404
  7.2 38.3 %copy-start.7 = (f32[1600]{0:T(1024)S(1)}, f32[1600]{0:T(1024)}, u32[]{:S(2)}) copy-start(f32[1600]{0:T(1024)} %param.25) | copy-start | bytes 19204
  7.2 38.3 %copy-start.6 = (f32[1600]{0:T(1024)S(1)}, f32[1600]{0:T(1024)}, u32[]{:S(2)}) copy-start(f32[1600]{0:T(1024)} %param.26) | copy-start | bytes 19204
  7.2 34.4 %all-gather.6.cloned.1.call-start = ((), (), s32[]{:S(2)}) async-start(), calls=%async_computation.6 | async-start | bytes 4096000 | tf_op jit(solution)/shard_map/all_gather | solution.py:97
  7.9 325.6 %all-gather.8.cloned.1.call-start = ((), (), s32[]{:S(2)}) async-start(), calls=%async_computation.7 | async-start | bytes 5990400 | tf_op jit(solution)/shard_map/all_gather | solution.py:101
  10.5 41.2 %all-to-all-start.1 = ((bf16[8,1,4]{2,1,0:T(2,128)(2,1)}), bf16[8,1,4]{2,1,0:T(2,128)(2,1)S(1)}, u32[]{:S(2)}, u32[]{:S(2)}) async-start(bf16[8,1,4]{2,1,0:T(2,128)(2,1)} %copy.30), calls=%async_computation.1 | async-start | bytes 8192 | tf_op jit(solution)/shard_map/all_to_all | solution.py:38
  41.6 2.9 copy-start.2
  51.7 134.4 %all-to-all-start = ((bf16[8,128,1600]{1,2,0:T(8,128)(2,1)}), bf16[8,128,1600]{1,2,0:T(8,128)(2,1)}, u32[]{:S(2)}, u32[]{:S(2)}) async-start(bf16[8,128,1600]{1,2,0:T(8,128)(2,1)} %copy.29), calls=%async_computation | async-start | bytes 6553600 | tf_op jit(solution)/shard_map/all_to_all | solution.py:37
  57.2 291.3 %all-gather.10.cloned.1.call-start = ((), (), s32[]{:S(2)}) async-start(), calls=%async_computation.8 | async-start | bytes 5990400 | tf_op jit(solution)/shard_map/all_gather | solution.py:117
  57.9 339.8 %reduce-scatter.2.cloned.1.call-start = ((), (), s32[]{:S(2)}) async-start(), calls=%async_computation.9 | async-start | bytes 4096000 | tf_op jit(solution)/shard_map/reduce_scatter | solution.py:120
  330.6 3.0 copy-start.11
  348.4 10.9 %copy-start.13 = (s32[8]{0:T(128)S(1)}, s32[8]{0:T(128)}, u32[]{:S(2)}) copy-start(s32[8]{0:T(128)} %param.35) | copy-start | bytes 100
  348.4 49.2 %copy-start.4 = (bf16[1024,400]{0,1:T(8,128)(2,1)S(1)}, bf16[1024,400]{0,1:T(8,128)(2,1)}, u32[]{:S(2)}) copy-start(bf16[1024,400]{0,1:T(8,128)(2,1)} %param.18) | copy-start | bytes 2457604
  348.4 49.3 %copy-start.10 = (f32[400]{0:T(512)S(1)}, f32[400]{0:T(512)}, u32[]{:S(2)}) copy-start(f32[400]{0:T(512)} %param.22) | copy-start | bytes 4804
  359.3 70.2 %all-gather.12.cloned.1.call-start = ((), (), s32[]{:S(2)}) async-start(), calls=%async_computation.10 | async-start | bytes 4096000 | tf_op jit(solution)/shard_map/all_gather | solution.py:125
  359.4 73.9 %copy-start.8 = (f32[1600]{0:T(1024)S(1)}, f32[1600]{0:T(1024)}, u32[]{:S(2)}) copy-start(f32[1600]{0:T(1024)} %param.28) | copy-start | bytes 19204
  359.4 73.9 %copy-start.9 = (f32[1600]{0:T(1024)S(1)}, f32[1600]{0:T(1024)}, u32[]{:S(2)}) copy-start(f32[1600]{0:T(1024)} %param.27) | copy-start | bytes 19204
  429.5 2.9 copy-start.3
  439.5 129.5 %copy-start.5 = (bf16[4,16,1600]{2,1,0:T(8,128)(2,1)S(1)}, bf16[4,16,1600]{2,1,0:T(8,128)(2,1)}, u32[]{:S(2)}) copy-start(bf16[4,16,1600]{2,1,0:T(8,128)(2,1)} %param.31) | copy-start | bytes 614404
  439.5 129.5 %all-to-all-start.3 = ((bf16[8,128,1600]{1,2,0:T(8,128)(2,1)}), bf16[8,128,1600]{1,2,0:T(8,128)(2,1)}, u32[]{:S(2)}, u32[]{:S(2)}) async-start(bf16[8,128,1600]{1,2,0:T(8,128)(2,1)} %copy.36), calls=%async_computation.4 | async-start | bytes 6553600 | tf_op jit(solution)/shard_map/all_to_all | solution.py:37
  445.1 191.2 %all-gather.14.cloned.1.call-start = ((), (), s32[]{:S(2)}) async-start(), calls=%async_computation.11 | async-start | bytes 4608000 | tf_op jit(solution)/shard_map/all_gather | solution.py:130
  633.9 2.4 copy-start.12
  636.3 10.9 %copy-start.1 = (bf16[4,16,1600]{2,1,0:T(8,128)(2,1)S(1)}, bf16[4,16,1600]{2,1,0:T(8,128)(2,1)}, u32[]{:S(2)}) copy-start(bf16[4,16,1600]{2,1,0:T(8,128)(2,1)} %param.30) | copy-start | bytes 614404
Sparse Core Ops, SparseCore 0:
  9.6 31.9 all-gather.5
  43.8 147.3 all-gather.7
  193.4 137.5 all-gather.9
  359.4 38.2 reduce-scatter.1
  400.2 29.2 all-gather.11
  448.1 123.5 all-gather.13
where the time goes:
time: 655 us; the launch traced here: 654 us
  waiting for transfers between devices  345 us (53%)
  blocking collectives  198 us (30%)
  matrix products  50.8 us (8%)
  other arithmetic  19.1 us (3%)
  starting transfers between devices  18.6 us (3%)
  between operations  14.3 us (2%)
  local copies, waits for them, and re-layouts  7.61 us (1%)
    all_to_all x2, waiting for transfers between devices, adapter_update(): lax.all_to_all(outgoing, 'row', split_axis=0, concat_axis=0, tiled=True)  251 us
    all_to_all x2, blocking collectives, adapter_update(): lax.all_to_all(answer, 'row', split_axis=0, concat_axis=0, tiled=True)  198 us
    reduce_scatter x1, waiting for transfers between devices, per_device(): lax.psum_scatter(partial_value.astype(jnp.bfloat16), 'col', scatter_dimen...  38.2 us
    all_gather x1, waiting for transfers between devices, per_device(): gathered_next = lax.all_gather(h_out, 'col', axis=1, tiled=True)  29.4 us
    dot_general x2, matrix products, fold_rows(): return jnp.dot(operand, weight_piece, preferred_element_type=jnp.float32)  25.8 us
    all_gather x1, waiting for transfers between devices, per_device(): gathered = lax.all_gather(hidden, 'col', axis=1, tiled=True)  23.9 us
  transfers between devices with their start and end apart: 9, of which 5 were waited for; matrix products, arithmetic and copies ran while one was open for 7% of the time, Pallas kernels for 0%

commit v1 on v0

--- a/solution.py
+++ b/solution.py
@@ -94,7 +94,12 @@
     valid = (jnp.arange(tile_len, dtype=jnp.int32)[None, :] < tile_token_rows[:, None]).reshape(
         tok_rows, 1
     )
-    gathered = lax.all_gather(hidden, "col", axis=1, tiled=True)
+    ring = [hidden]
+    for hop in range(3):
+        ring.append(lax.ppermute(ring[-1], "col", [(dev, (dev + 1) % 4) for dev in range(4)]))
+    gathered = jnp.roll(
+        jnp.concatenate(ring[::-1], axis=1), (lax.axis_index("col") + 1) * ring[0].shape[1], axis=1
+    )
     normalized_input = layer_norm(
         gathered.astype(jnp.float32), block_norm_gain, block_norm_shift
     ).astype(jnp.bfloat16)

time: 655 us -> 646 us (0.986)
  waiting for transfers between devices: 345 us -> 335 us
  blocking collectives: 198 us -> 190 us
    ppermute x0 -> x3, waiting for transfers between devices: none -> 27.3 us  [per_device(): lax.ppermute(ring[-1], 'col', [(dev, (dev + 1) % 4) for dev in range(4)])]
    all_gather x1 -> x0, waiting for transfers between devices: 23.9 us -> none  [per_device(): gathered = lax.all_gather(hidden, 'col', axis=1, tiled=True)]
    all_to_all x2, waiting for transfers between devices: 251 us -> 240 us  [adapter_update(): lax.all_to_all(outgoing, 'row', split_axis=0, concat_axis=0, tiled=True)]
    all_to_all x2, blocking collectives: 198 us -> 190 us  [adapter_update(): lax.all_to_all(answer, 'row', split_axis=0, concat_axis=0, tiled=True)]
  transfers between devices with their start and end apart: 9 -> 11, of which waited for: 5 -> 7; matrix products, arithmetic and copies ran while one was open for 7% -> 7% of each run, Pallas kernels for 0% -> 0%
where the time goes in v1:
time: 646 us; the launch traced here: 639 us
  waiting for transfers between devices  335 us (52%)
  blocking collectives  190 us (29%)
  matrix products  51.2 us (8%)
  other arithmetic  20.2 us (3%)
  starting transfers between devices  19.4 us (3%)
  between operations  14.3 us (2%)
  local copies, waits for them, and re-layouts  9.18 us (1%)
    all_to_all x2, waiting for transfers between devices, adapter_update(): lax.all_to_all(outgoing, 'row', split_axis=0, concat_axis=0, tiled=True)  240 us
    all_to_all x2, blocking collectives, adapter_update(): lax.all_to_all(answer, 'row', split_axis=0, concat_axis=0, tiled=True)  190 us
    reduce_scatter x1, waiting for transfers between devices, per_device(): lax.psum_scatter(partial_value.astype(jnp.bfloat16), 'col', scatter_dimen...  37 us
    all_gather x1, waiting for transfers between devices, per_device(): gathered_next = lax.all_gather(h_out, 'col', axis=1, tiled=True)  29.4 us
    dot_general x2, matrix products, fold_rows(): return jnp.dot(operand, weight_piece, preferred_element_type=jnp.float32)  27.3 us
    ppermute x3, waiting for transfers between devices, per_device(): lax.ppermute(ring[-1], 'col', [(dev, (dev + 1) % 4) for dev in range(4)])  27.3 us
  transfers between devices with their start and end apart: 11, of which 7 were waited for; matrix products, arithmetic and copies ran while one was open for 7% of the time, Pallas kernels for 0%

profile of v1, /device:TPU:0, one launch (start us, length us, event | category | flops | bytes accessed | tf_op | source)
XLA Modules:
  0.0 638.7 jit_solution(15890471128266679269)
XLA Ops:
  7.2 0.5 collective-permute-start
  7.7 12.2 %collective-permute-done = bf16[1024,400]{0,1:T(8,128)(2,1)S(1)} collective-permute-done((bf16[1024,400]{0,1:T(8,128)(2,1)}, bf16[1024,400]{0,1:T(8,128)(2,1)S(1)}, u32[]{:S(2)}, u32[]{:S(2)}) %collective-permute-start) | collective-permute-done | bytes 819232 | tf_op jit(solution)/shard_map/ppermute | solution.py:99
  20.0 11.7 %collective-permute-done.1 = bf16[1024,400]{0,1:T(8,128)(2,1)S(1)} collective-permute-done((bf16[1024,400]{0,1:T(8,128)(2,1)S(1)}, bf16[1024,400]{0,1:T(8,128)(2,1)S(1)}, u32[]{:S(2)}, u32[]{:S(2)}) %collective-permute-start.1) | collective-permute-done | bytes 819232 | tf_op jit(solution)/shard_map/ppermute | solution.py:99
  31.7 0.9 select_reduce_fusion
  32.6 0.3 fusion.48
  32.8 0.7 copy.30
  33.5 6.6 %all-to-all-start.1 = ((bf16[8,1,4]{2,1,0:T(2,128)(2,1)}), bf16[8,1,4]{2,1,0:T(2,128)(2,1)S(1)}, u32[]{:S(2)}, u32[]{:S(2)}) async-start(bf16[8,1,4]{2,1,0:T(2,128)(2,1)} %copy.30), calls=%async_computation.1 | async-start | bytes 8192 | tf_op jit(solution)/shard_map/all_to_all | solution.py:38
  40.1 3.4 collective-permute-done.2
  43.7 1.2 constant_dynamic-update-slice_fusion.4
  45.2 1.0 convert_reduce_fusion.1
  46.1 1.3 fusion.8
  47.5 0.4 copy-done.3
  47.9 2.1 fusion.77
  49.9 0.9 copy.46
  50.8 1.4 convolution_convert_fusion.2
  52.2 2.3 copy.29
  54.5 6.6 %all-to-all-start = ((bf16[8,128,1600]{1,2,0:T(8,128)(2,1)}), bf16[8,128,1600]{1,2,0:T(8,128)(2,1)S(1)}, u32[]{:S(2)}, u32[]{:S(2)}) async-start(bf16[8,128,1600]{1,2,0:T(8,128)(2,1)} %copy.29), calls=%async_computation | async-start | bytes 6553600 | tf_op jit(solution)/shard_map/all_to_all | solution.py:37
  61.1 0.7 all-gather.7.cloned.1.call-update
  61.9 0.1 copy.31
  62.0 0.1 copy.32
  62.1 0.1 copy.33
  62.2 116.4 %all-to-all-done = bf16[8,128,1600]{1,2,0:T(8,128)(2,1)S(1)} async-done(((bf16[8,128,1600]{1,2,0:T(8,128)(2,1)}), bf16[8,128,1600]{1,2,0:T(8,128)(2,1)S(1)}, u32[]{:S(2)}, u32[]{:S(2)}) %all-to-all-start) | async-done | bytes 3276832 | tf_op jit(solution)/shard_map/all_to_all | solution.py:37
  178.6 1.6 fusion.45
  180.3 1.1 bitcast_convert_fusion
  181.4 129.8 %all_to_all.33 = bf16[8,128,1600]{1,2,0:T(8,128)(2,1)S(1)} all-to-all(bf16[8,128,1600]{1,2,0:T(8,128)(2,1)S(1)} %bitcast_convert_fusion), channel_id=1, replica_groups=mesh['row'=8,'col'=4] {'row'}, dimensions={0} | all-to-all | bytes 6553600 | tf_op jit(solution)/shard_map/all_to_all | solution.py:55
  311.2 2.0 fusion.30
  313.2 3.0 convert_element_type.115
  316.2 16.4 %fusion.19.clone.4 = bf16[1024,1600]{0,1:T(8,128)(2,1)} fusion(f32[200,8,8,128]{3,2,1,0:T(8,128)} %bitcast.93, bf16[1600,1600]{1,0:T(8,128)(2,1)} %all-gather.5.cloned.1.call-done, f32[1600]{0:T(1024)S(1)} %copy-done.12, f32[1600]{0:T(1024)S(1)} %copy-done.7, f32[1600]{0:T(1024)S(1)} %copy-done.8, f32[1024]{0:T(1024)S(1)} %add_rsqrt_fusion.1, ...), kind=kOutput, calls=%fused_computation.24.clone.clone.clone.1 | convolution fusion | flops 5270732800 | bytes 18459396 | tf_op jit(solution)/shard_map/dot_general | solution.py:15
  332.7 10.8 %convolution_convert_fusion = bf16[1024,1600]{0,1:T(8,128)(2,1)} fusion(bf16[1600,1600]{0,1:T(8,128)(2,1)} %all-gather.7.cloned.1.call-done, bf16[1024,1600]{0,1:T(8,128)(2,1)} %fusion.19.clone.4), kind=kOutput, calls=%fused_computation.31 | convolution fusion | flops 5244518400 | bytes 11673600 | tf_op jit(solution)/shard_map/dot_general | solution.py:120
  343.5 0.1 fusion.64
  343.6 37.0 %reduce-scatter.2.cloned.1.call-done = bf16[1024,400]{0,1:T(8,128)(2,1)} async-done(((bf16[1024,1600]{0,1:T(8,128)(2,1)}), bf16[1024,400]{0,1:T(8,128)(2,1)}) %reduce-scatter.2.cloned.1.call-update) | async-done | bytes 819216 | tf_op jit(solution)/shard_map/reduce_scatter | solution.py:125
  380.6 2.3 select_convert_fusion
  383.0 29.4 %all-gather.9.cloned.1.call-done = bf16[1024,1600]{0,1:T(8,128)(2,1)} async-done(((bf16[1024,400]{0,1:T(8,128)(2,1)}), bf16[1024,1600]{0,1:T(8,128)(2,1)}) %all-gather.9.cloned.1.call-update) | async-done | bytes 3276816 | tf_op jit(solution)/shard_map/all_gather | solution.py:130
  412.4 2.7 convert_reduce_fusion
  415.1 2.8 fusion.4
  418.0 1.6 fusion.75
  419.6 0.9 copy.48
  420.5 1.4 convolution_convert_fusion.1
  422.0 2.2 copy.36
  424.2 5.5 all-to-all-start.3
  429.7 0.5 all-gather.11.cloned.1.call-update
  430.3 123.2 %all-to-all-done.3 = bf16[8,128,1600]{1,2,0:T(8,128)(2,1)} async-done(((bf16[8,128,1600]{1,2,0:T(8,128)(2,1)}), bf16[8,128,1600]{1,2,0:T(8,128)(2,1)}, u32[]{:S(2)}, u32[]{:S(2)}) %all-to-all-start.3) | async-done | bytes 3276832 | tf_op jit(solution)/shard_map/all_to_all | solution.py:37
  553.5 2.6 fusion.42
  556.1 1.8 bitcast_convert_fusion.1
  557.9 59.8 %all_to_all.34 = bf16[8,128,1200]{1,2,0:T(8,128)(2,1)S(1)} all-to-all(bf16[8,128,1200]{1,2,0:T(8,128)(2,1)S(1)} %bitcast_convert_fusion.1), channel_id=1, replica_groups=mesh['row'=8,'col'=4] {'row'}, dimensions={0} | all-to-all | bytes 4915200 | tf_op jit(solution)/shard_map/all_to_all | solution.py:55
  617.8 0.8 fusion.33
  618.6 2.4 convert_element_type.116
  621.0 10.9 %fusion.21 = bf16[1024,1200]{0,1:T(8,128)(2,1)} fusion(f32[150,8,8,128]{3,2,1,0:T(8,128)} %bitcast.94, bf16[1600,1200]{1,0:T(8,128)(2,1)} %all-gather.11.cloned.1.call-done, f32[1200]{0:T(1024)S(1)} %copy-done.13, pred[1024]{0:T(1024)(128)(4,1)S(1)} %fusion.64, bf16[1024,1600]{0,1:T(8,128)(2,1)S(1)} %copy-done.2, f32[1600]{0:T(1024)S(1)} %copy-done.9, ...), kind=kOutput, calls=%fused_computation.29 | convolution fusion | flops 3946905600 | bytes 14516416 | tf_op jit(solution)/shard_map/dot_general | solution.py:15
  (56 shorter events, 0.8 us)
Async XLA Ops:
  7.2 173.1 %copy-start = (bf16[4,16,1600]{2,1,0:T(8,128)(2,1)S(1)}, bf16[4,16,1600]{2,1,0:T(8,128)(2,1)}, u32[]{:S(2)}) copy-start(bf16[4,16,1600]{2,1,0:T(8,128)(2,1)} %param.30) | copy-start | bytes 614404
  7.2 37.9 %copy-start.4 = (bf16[1024,400]{0,1:T(8,128)(2,1)S(1)}, bf16[1024,400]{0,1:T(8,128)(2,1)}, u32[]{:S(2)}) copy-start(bf16[1024,400]{0,1:T(8,128)(2,1)} %param.18) | copy-start | bytes 2457604
  7.2 309.0 %all-gather.5.cloned.1.call-start = ((), (), s32[]{:S(2)}) async-start(), calls=%async_computation.6 | async-start | bytes 5990400 | tf_op jit(solution)/shard_map/all_gather | solution.py:106
  7.2 12.7 %collective-permute-start = (bf16[1024,400]{0,1:T(8,128)(2,1)}, bf16[1024,400]{0,1:T(8,128)(2,1)S(1)}, u32[]{:S(2)}, u32[]{:S(2)}) collective-permute-start(bf16[1024,400]{0,1:T(8,128)(2,1)} %param.18), channel_id=1, source_target_pairs={{0,1},{1,2},{2,3},{3,0},{4,5},{5,6},{6,7},{7,4},{8,9},{9,10},{10,1... | collective-permute-start | bytes 2457608 | tf_op jit(solution)/shard_map/ppermute | solution.py:99
  19.9 11.8 %collective-permute-start.1 = (bf16[1024,400]{0,1:T(8,128)(2,1)S(1)}, bf16[1024,400]{0,1:T(8,128)(2,1)S(1)}, u32[]{:S(2)}, u32[]{:S(2)}) collective-permute-start(bf16[1024,400]{0,1:T(8,128)(2,1)S(1)} %collective-permute-done), channel_id=1, source_target_pairs={{0,1},{1,2},{2,3},{3,0},{4,5},{5,6},{6,7},{7,4},{8,9},{9,10},{10,1... | collective-permute-start | bytes 2457608 | tf_op jit(solution)/shard_map/ppermute | solution.py:99
  31.7 11.8 %collective-permute-start.2 = (bf16[1024,400]{0,1:T(8,128)(2,1)S(1)}, bf16[1024,400]{0,1:T(8,128)(2,1)S(1)}, u32[]{:S(2)}, u32[]{:S(2)}) collective-permute-start(bf16[1024,400]{0,1:T(8,128)(2,1)S(1)} %collective-permute-done.1), channel_id=1, source_target_pairs={{0,1},{1,2},{2,3},{3,0},{4,5},{5,6},{6,7},{7,4},{8,9},{9,10},{10,1... | collective-permute-start | bytes 2457608 | tf_op jit(solution)/shard_map/ppermute | solution.py:99
  33.5 21.0 %all-to-all-start.1 = ((bf16[8,1,4]{2,1,0:T(2,128)(2,1)}), bf16[8,1,4]{2,1,0:T(2,128)(2,1)S(1)}, u32[]{:S(2)}, u32[]{:S(2)}) async-start(bf16[8,1,4]{2,1,0:T(2,128)(2,1)} %copy.30), calls=%async_computation.1 | async-start | bytes 8192 | tf_op jit(solution)/shard_map/all_to_all | solution.py:38
  44.9 3.0 copy-start.7
  44.9 3.0 copy-start.8
  45.1 2.7 copy-start.3
  54.5 124.1 %all-to-all-start = ((bf16[8,128,1600]{1,2,0:T(8,128)(2,1)}), bf16[8,128,1600]{1,2,0:T(8,128)(2,1)S(1)}, u32[]{:S(2)}, u32[]{:S(2)}) async-start(bf16[8,128,1600]{1,2,0:T(8,128)(2,1)} %copy.29), calls=%async_computation | async-start | bytes 6553600 | tf_op jit(solution)/shard_map/all_to_all | solution.py:37
  61.1 271.6 %all-gather.7.cloned.1.call-start = ((), (), s32[]{:S(2)}) async-start(), calls=%async_computation.7 | async-start | bytes 5990400 | tf_op jit(solution)/shard_map/all_gather | solution.py:122
  61.8 318.8 %reduce-scatter.2.cloned.1.call-start = ((), (), s32[]{:S(2)}) async-start(), calls=%async_computation.8 | async-start | bytes 4096000 | tf_op jit(solution)/shard_map/reduce_scatter | solution.py:125
  313.2 3.0 copy-start.12
  332.6 10.9 %copy-start.14 = (s32[8]{0:T(128)S(1)}, s32[8]{0:T(128)}, u32[]{:S(2)}) copy-start(s32[8]{0:T(128)} %param.35) | copy-start | bytes 100
  332.6 48.0 %copy-start.5 = (bf16[1024,400]{0,1:T(8,128)(2,1)S(1)}, bf16[1024,400]{0,1:T(8,128)(2,1)}, u32[]{:S(2)}) copy-start(bf16[1024,400]{0,1:T(8,128)(2,1)} %param.18) | copy-start | bytes 2457604
  332.6 48.0 %copy-start.11 = (f32[400]{0:T(512)S(1)}, f32[400]{0:T(512)}, u32[]{:S(2)}) copy-start(f32[400]{0:T(512)} %param.22) | copy-start | bytes 4804
  343.4 74.5 %copy-start.9 = (f32[1600]{0:T(1024)S(1)}, f32[1600]{0:T(1024)}, u32[]{:S(2)}) copy-start(f32[1600]{0:T(1024)} %param.28) | copy-start | bytes 19204
  343.4 74.6 %copy-start.10 = (f32[1600]{0:T(1024)S(1)}, f32[1600]{0:T(1024)}, u32[]{:S(2)}) copy-start(f32[1600]{0:T(1024)} %param.27) | copy-start | bytes 19204
  343.4 69.0 %all-gather.9.cloned.1.call-start = ((), (), s32[]{:S(2)}) async-start(), calls=%async_computation.9 | async-start | bytes 4096000 | tf_op jit(solution)/shard_map/all_gather | solution.py:130
  412.4 5.6 copy-start.2
  421.9 131.5 %copy-start.6 = (bf16[4,16,1600]{2,1,0:T(8,128)(2,1)S(1)}, bf16[4,16,1600]{2,1,0:T(8,128)(2,1)}, u32[]{:S(2)}) copy-start(bf16[4,16,1600]{2,1,0:T(8,128)(2,1)} %param.31) | copy-start | bytes 614404
  424.2 129.3 %all-to-all-start.3 = ((bf16[8,128,1600]{1,2,0:T(8,128)(2,1)}), bf16[8,128,1600]{1,2,0:T(8,128)(2,1)}, u32[]{:S(2)}, u32[]{:S(2)}) async-start(bf16[8,128,1600]{1,2,0:T(8,128)(2,1)} %copy.36), calls=%async_computation.4 | async-start | bytes 6553600 | tf_op jit(solution)/shard_map/all_to_all | solution.py:37
  429.7 191.4 %all-gather.11.cloned.1.call-start = ((), (), s32[]{:S(2)}) async-start(), calls=%async_computation.10 | async-start | bytes 4608000 | tf_op jit(solution)/shard_map/all_gather | solution.py:135
  617.8 3.3 copy-start.13
  621.0 10.9 %copy-start.1 = (bf16[4,16,1600]{2,1,0:T(8,128)(2,1)S(1)}, bf16[4,16,1600]{2,1,0:T(8,128)(2,1)}, u32[]{:S(2)}) copy-start(bf16[4,16,1600]{2,1,0:T(8,128)(2,1)} %param.30) | copy-start | bytes 614404
Sparse Core Ops, SparseCore 0:
  20.1 143.1 all-gather.4
  165.5 141.3 all-gather.6
  343.6 36.9 reduce-scatter.1
  383.1 29.2 all-gather.8
  432.6 123.5 all-gather.10
